TPU v7x, 32 devices: a whole 2x2x4 slice. The times are simulated.
32 devices in a mesh: groups: 2 (over y), ctx: 16 (over z, x, core).
Axes of the slice: x: 2, y: 2, z: 4, core: 2. Of those that a mesh axis runs over, the one named last changes fastest.
Arguments:
- inputs: bfloat16 [8192, 1024], P(('groups', 'ctx')), parts along dimension 0, may hold values from -6 to 6
- out_grad: bfloat16 [8192, 1024], P(('groups', 'ctx')), parts along dimension 0, may hold values from -6 to 6
- filter_taps: float32 [2048, 1024], P('groups'), parts along dimension 0, may hold values from -0.1875 to 0.1875
- block_owner: int32 [16], replicated, may hold values from 0 to 15, each once
Outputs:
- input_grad: bfloat16 [8192, 1024], P(('groups', 'ctx')), parts along dimension 0
- filter_grad: float32 [2048, 1024], P(('groups', 'ctx')), parts along dimension 0
There are 2 independent parts, one for each index of `groups`. A program takes and returns all parts, laid end to end along the dimension named above; an argument that names none is the same for every part. Nothing has to cross between parts.
Inputs may be any that keep to these rules, and one draw needn't show every extreme that they name: block_owner names every ctx index exactly once.
All inputs are finite; a program needn't handle non-finite values.
Results may differ from a plain program's by a relative error of at most 0.007.
Values may be sent and summed in bfloat16 or wider, within the bound.
A program may use at most 128 MiB of HBM per device.

v0:
```python
import functools
import math

import jax
import jax.numpy as jnp
import ml_dtypes
import numpy as np
from jax import lax
from jax.experimental import pallas as pl
from jax.experimental.pallas import tpu as pltpu
from jax.sharding import PartitionSpec as P

MESH = pl.DeviceIdType.MESH
ROWS = 16
LANES = 128


def make_tables(block):
    order = np.concatenate([np.arange(0, block, 2), np.arange(1, block, 2)]).astype(np.int64)
    place = np.arange(block, dtype=np.int64)
    period = 4 * block
    ahead = ((2 * order + 1)[:, None] * place[None, :]) % period
    ahead = ahead * (2.0 * math.pi / period)
    forward = np.concatenate([np.cos(ahead), -np.sin(ahead)], axis=0)
    inverse = np.concatenate([np.cos(ahead), -np.sin(ahead)], axis=0).T / block
    behind = ((2 * order + 1)[:, None] * (block - place)[None, :]) % period
    behind = behind * (2.0 * math.pi / period)
    backward = np.concatenate([np.cos(behind), -np.sin(behind)], axis=0).T / block
    return [t.astype(np.float32).astype(ml_dtypes.bfloat16) for t in (forward, inverse, backward)]


def kernel(
    gang,
    planes,
    scale,
    holder_ref,
    fwd_ref,
    inv_ref,
    back_ref,
    x_ref,
    g_ref,
    taps_ref,
    o_ref,
    f_ref,
    xbuf,
    gbuf,
    taps,
    xspec,
    gspec,
    fspec,
    prod,
    lag,
    outbuf,
    lag_send,
    lag_recv,
    lag_sum,
    local_sem,
    x_send,
    x_recv,
    g_send,
    g_recv,
    xh_send,
    xh_recv,
    gh_send,
    gh_recv,
    o_send,
    o_recv,
    l_send,
    l_recv,
    f_send,
    f_recv,
):
    me = lax.axis_index("ctx")
    q = me // gang
    j = me % gang
    block, width = xbuf.shape[2], xbuf.shape[3]
    lag_block = f_ref.shape[0]
    half = block // 2

    def peer(d):
        found = 0
        bit = 1
        while bit < gang:
            found = found + ((j // bit + d // bit) % 2) * bit
            bit *= 2
        return found

    def cols(at):
        return pl.ds(pl.multiple_of(at * width, width), width)

    def remote(src, dst, send, recv, plane, at):
        return pltpu.make_async_remote_copy(
            src_ref=src,
            dst_ref=dst,
            send_sem=send,
            recv_sem=recv,
            device_id={"ctx": plane * gang + at},
            device_id_type=MESH,
        )

    own_x = pltpu.make_async_copy(x_ref.at[:, cols(j)], xbuf.at[1, j], local_sem.at[0])
    own_g = pltpu.make_async_copy(g_ref.at[:, cols(j)], gbuf.at[0, j], local_sem.at[1])
    own_taps = pltpu.make_async_copy(taps_ref.at[:, cols(j)], taps, local_sem.at[2])
    own_x.start()
    own_g.start()
    own_taps.start()

    barrier = pltpu.get_barrier_semaphore()
    for d in range(1, gang):
        pl.semaphore_signal(
            barrier, inc=1, device_id={"ctx": q * gang + peer(d)}, device_id_type=MESH
        )
    for e in range(1, planes):
        pl.semaphore_signal(
            barrier, inc=1, device_id={"ctx": ((q + e) % planes) * gang + j}, device_id_type=MESH
        )
    pl.semaphore_wait(barrier, gang - 1 + planes - 1)

    def x_copy(d):
        return remote(
            x_ref.at[:, cols(peer(d))], xbuf.at[1, j], x_send.at[d], x_recv.at[d], q, peer(d)
        )

    def g_copy(d):
        return remote(
            g_ref.at[:, cols(peer(d))], gbuf.at[0, j], g_send.at[d], g_recv.at[d], q, peer(d)
        )

    def x_ahead(d):
        source = x_ref.at[:, cols(j)] if d == 0 else xbuf.at[1, peer(d)]
        return remote(
            source, xbuf.at[0, peer(d)], xh_send.at[d], xh_recv.at[d], (q + 1) % planes, j
        )

    def g_ahead(d):
        source = g_ref.at[:, cols(j)] if d == 0 else gbuf.at[0, peer(d)]
        return remote(
            source,
            gbuf.at[1, peer(d)],
            gh_send.at[d],
            gh_recv.at[d],
            (q + planes - 1) % planes,
            j,
        )

    def arrived(ref, sem, at):
        remote(ref, ref, sem, sem, q, at).wait_recv()

    for d in reversed(range(1, gang)):
        x_copy(d).start()
        g_copy(d).start()

    @pl.when(q + 1 < planes)
    def _():
        x_ahead(0).start()

    @pl.when(q > 0)
    def _():
        g_ahead(0).start()

    @pl.when(q == 0)
    def _():
        xbuf[0] = jnp.zeros(xbuf.shape[1:], xbuf.dtype)

    @pl.when(q == planes - 1)
    def _():
        gbuf[1] = jnp.zeros(gbuf.shape[1:], gbuf.dtype)

    def spectrum(value):
        return jnp.dot(fwd_ref[...], value, preferred_element_type=jnp.float32)

    for d in range(1, gang):
        arrived(xbuf.at[1, peer(d)], x_recv.at[d], peer(d))

        @pl.when(q + 1 < planes)
        def _():
            x_ahead(d).start()

        arrived(gbuf.at[0, peer(d)], g_recv.at[d], peer(d))

        @pl.when(q > 0)
        def _():
            g_ahead(d).start()

    own_taps.wait()

    @pl.loop(0, gang)
    def _(t):
        rows = pl.ds(pl.multiple_of(t * block, block), block)
        fspec[t] = spectrum(taps[rows, :].astype(jnp.bfloat16))

    own_x.wait()
    own_g.wait()

    @pl.loop(0, gang)
    def _(t):
        xspec[gang + t] = spectrum(xbuf[1, t])
        gspec[t] = spectrum(gbuf[0, t])

    @pl.when(q > 0)
    def _():
        for d in range(gang):
            arrived(xbuf.at[0, peer(d)], xh_recv.at[d], j)

    @pl.loop(0, gang)
    def _(t):
        xspec[t] = spectrum(xbuf[0, t])

    def tiles(body):
        for part, sign in ((0, 1.0), (1, -1.0)):
            for lane in range(width // LANES):

                @pl.loop(0, half // ROWS)
                def _(step):
                    first = pl.multiple_of(part * half + step * ROWS, ROWS)
                    second = pl.multiple_of(block + part * half + step * ROWS, ROWS)
                    at = pl.ds(lane * LANES, LANES)
                    body(pl.ds(first, ROWS), pl.ds(second, ROWS), at, sign)

    def windows(spec, real, imag, at, sign):
        parts = [(spec[w, real, at], spec[w, imag, at]) for w in range(2 * gang)]
        found = []
        for w in range(2 * gang - 1):
            low, high = parts[w], parts[w + 1]
            if sign > 0:
                found.append((low[0] + high[1], low[1] - high[0]))
            else:
                found.append((low[0] - high[1], low[1] + high[0]))
        return found

    def lag_tile(real, imag, at, sign):
        window = windows(xspec, real, imag, at, sign)
        own = [(gspec[t, real, at], gspec[t, imag, at]) for t in range(gang)]
        for o in range(gang):
            total_r, total_i = None, None
            for t in range(gang):
                a, b = own[t], window[gang + t - o - 1]
                r = a[0] * b[0] + a[1] * b[1]
                i = a[0] * b[1] - a[1] * b[0]
                total_r = r if total_r is None else total_r + r
                total_i = i if total_i is None else total_i + i
            prod[o, real, at] = total_r.astype(jnp.bfloat16)
            prod[o, imag, at] = total_i.astype(jnp.bfloat16)

    tiles(lag_tile)

    @pl.loop(0, gang)
    def _(o):
        found = jnp.dot(back_ref[...], prod[o], preferred_element_type=jnp.float32)
        count = block // lag_block
        lag[pl.ds(o * count, count)] = found.reshape(count, lag_block, width)

    def lag_copy(e):
        to = (q + e) % planes
        return remote(lag_send.at[to], lag_recv.at[q], l_send.at[e], l_recv.at[e], to, j)

    for e in range(planes):
        to = (q + e + 1) % planes
        pieces = []
        for at in range(gang):
            pieces.append(lag[holder_ref[to * gang + at]])
        whole = jnp.concatenate(pieces, axis=0)
        if e < planes - 1:
            lag_send[to] = whole.astype(jnp.bfloat16)
            lag_copy(e + 1).start()
        else:
            lag_sum[...] = whole

    @pl.when(q < planes - 1)
    def _():
        for d in range(gang):
            arrived(gbuf.at[1, peer(d)], gh_recv.at[d], j)

    @pl.loop(0, gang)
    def _(t):
        gspec[gang + t] = spectrum(gbuf[1, t])

    def grad_tile(real, imag, at, sign):
        window = windows(gspec, real, imag, at, sign)
        own = [(fspec[o, real, at], fspec[o, imag, at]) for o in range(gang)]
        for t in range(gang):
            total_r, total_i = None, None
            for o in range(gang):
                a, b = own[o], window[t + o]
                r = a[0] * b[0] + a[1] * b[1]
                i = a[0] * b[1] - a[1] * b[0]
                total_r = r if total_r is None else total_r + r
                total_i = i if total_i is None else total_i + i
            prod[t, real, at] = total_r.astype(jnp.bfloat16)
            prod[t, imag, at] = total_i.astype(jnp.bfloat16)

    tiles(grad_tile)

    def o_copy(d):
        return remote(
            outbuf.at[peer(d)], o_ref.at[:, cols(j)], o_send.at[d], o_recv.at[d], q, peer(d)
        )

    own_o = pltpu.make_async_copy(outbuf.at[j], o_ref.at[:, cols(j)], local_sem.at[3])
    for d in list(range(gang - 1, 0, -1)) + [0]:
        at = peer(d)
        outbuf[at] = jnp.dot(inv_ref[...], prod[at], preferred_element_type=jnp.float32).astype(
            jnp.bfloat16
        )
        if d > 0:
            o_copy(d).start()
        else:
            own_o.start()

    for e in range(1, planes):
        source = (q + planes - e) % planes
        remote(
            lag_recv.at[source], lag_recv.at[source], l_recv.at[e], l_recv.at[e], source, j
        ).wait_recv()
        lag_sum[...] = lag_sum[...] + lag_recv[source].astype(jnp.float32)
    lag_sum[...] = lag_sum[...] * scale

    def lag_rows(at):
        return lag_sum.at[pl.ds(pl.multiple_of(at * lag_block, lag_block), lag_block), :]

    def f_copy(d):
        return remote(
            lag_rows(peer(d)), f_ref.at[:, cols(j)], f_send.at[d], f_recv.at[d], q, peer(d)
        )

    own_f = pltpu.make_async_copy(lag_rows(j), f_ref.at[:, cols(j)], local_sem.at[4])
    for d in reversed(range(1, gang)):
        f_copy(d).start()
    own_f.start()

    for d in range(1, gang):
        arrived(o_ref.at[:, cols(peer(d))], o_recv.at[d], peer(d))
        arrived(f_ref.at[:, cols(peer(d))], f_recv.at[d], peer(d))
        x_copy(d).wait_send()
        g_copy(d).wait_send()
        o_copy(d).wait_send()
        f_copy(d).wait_send()
    for e in range(1, planes):
        lag_copy(e).wait_send()

    @pl.when(q + 1 < planes)
    def _():
        for d in range(gang):
            x_ahead(d).wait_send()

    @pl.when(q > 0)
    def _():
        for d in range(gang):
            g_ahead(d).wait_send()

    own_o.wait()
    own_f.wait()


def shards(inputs, out_grad, filter_taps, block_owner):
    block, channels = inputs.shape
    devices = lax.axis_size("ctx")
    lags = filter_taps.shape[0]
    gang = lags // block
    planes = devices // gang
    width = channels // gang
    lag_block = lags // devices
    scale = 1.0 / math.sqrt(devices * block)
    ids = jnp.arange(devices, dtype=jnp.int32)
    holder = jnp.sum(
        jnp.where(block_owner[None, :] == ids[:, None], ids[None, :], 0), axis=1, dtype=jnp.int32
    )
    forward, inverse, backward = [jnp.asarray(t) for t in make_tables(block)]
    vmem = pl.BlockSpec(memory_space=pltpu.VMEM)
    hbm = pl.BlockSpec(memory_space=pl.ANY)
    dma = pltpu.SemaphoreType.DMA
    return pl.pallas_call(
        functools.partial(kernel, gang, planes, scale),
        out_shape=(
            jax.ShapeDtypeStruct((block, channels), jnp.bfloat16),
            jax.ShapeDtypeStruct((lag_block, channels), jnp.float32),
        ),
        in_specs=[pl.BlockSpec(memory_space=pltpu.SMEM)] + [vmem] * 3 + [hbm] * 3,
        out_specs=(hbm, hbm),
        scratch_shapes=[
            pltpu.VMEM((2, gang, block, width), jnp.bfloat16),
            pltpu.VMEM((2, gang, block, width), jnp.bfloat16),
            pltpu.VMEM((lags, width), jnp.float32),
            pltpu.VMEM((2 * gang, 2 * block, width), jnp.float32),
            pltpu.VMEM((2 * gang, 2 * block, width), jnp.float32),
            pltpu.VMEM((gang, 2 * block, width), jnp.float32),
            pltpu.VMEM((gang, 2 * block, width), jnp.bfloat16),
            pltpu.VMEM((devices, lag_block, width), jnp.float32),
            pltpu.VMEM((gang, block, width), jnp.bfloat16),
            pltpu.VMEM((planes, gang * lag_block, width), jnp.bfloat16),
            pltpu.VMEM((planes, gang * lag_block, width), jnp.bfloat16),
            pltpu.VMEM((gang * lag_block, width), jnp.float32),
            dma((5,)),
        ]
        + [dma((gang,))] * 10
        + [dma((planes,))] * 2
        + [dma((gang,))] * 2,
        compiler_params=pltpu.CompilerParams(
            collective_id=0, has_side_effects=True, vmem_limit_bytes=44 * 1024 * 1024
        ),
    )(holder, forward, inverse, backward, inputs, out_grad, filter_taps)


def solution(mesh):
    placed = (P(("groups", "ctx"), None), P(("groups", "ctx"), None), P("groups", None), P())
    return jax.shard_map(
        shards,
        mesh=mesh,
        in_specs=placed,
        out_specs=(P(("groups", "ctx"), None), P(("groups", "ctx"), None)),
        check_vma=False,
    )
```

profile of v0, /device:TPU:14, one launch (start us, length us, event | category | flops | bytes accessed | tf_op | source)
XLA Modules:
  0.0 51.8 jit_solution(333529211769642489)
XLA Ops:
  0.6 0.8 %select_reduce_fusion.holder_ref = s32[16]{0:T(128)S(1)} fusion(s32[16]{0:T(128)} %param.10), kind=kLoop, calls=%fused_computation | loop fusion | flops 752 | bytes 128 | tf_op jit(solution)/shard_map/reduce_sum | solution.py:365
  1.4 0.0 copy-start
  1.4 2.2 %copy-done = f32[1024,1024]{1,0:T(8,128)S(1)} copy-done((f32[1024,1024]{1,0:T(8,128)S(1)}, f32[1024,1024]{1,0:T(8,128)}, u32[]{:S(2)}) %copy-start) | copy-done | bytes 4194328
  3.6 0.0 copy-start.1
  3.6 1.0 %copy-done.1 = bf16[256,1024]{1,0:T(8,128)(2,1)S(1)} copy-done((bf16[256,1024]{1,0:T(8,128)(2,1)S(1)}, bf16[256,1024]{1,0:T(8,128)(2,1)}, u32[]{:S(2)}) %copy-start.1) | copy-done | bytes 524312
  4.6 0.0 copy-start.2
  4.6 1.0 %copy-done.2 = bf16[256,1024]{1,0:T(8,128)(2,1)S(1)} copy-done((bf16[256,1024]{1,0:T(8,128)(2,1)S(1)}, bf16[256,1024]{1,0:T(8,128)(2,1)}, u32[]{:S(2)}) %copy-start.2) | copy-done | bytes 524312
  5.7 0.0 copy-start.3
  5.7 0.9 %copy-done.3 = bf16[256,512]{1,0:T(8,128)(2,1)S(1)} copy-done((bf16[256,512]{1,0:T(8,128)(2,1)S(1)}, bf16[256,512]{1,0:T(8,128)(2,1)}, u32[]{:S(2)}) %copy-start.3) | copy-done | bytes 262168
  6.6 0.0 copy-start.4
  6.6 0.9 %copy-done.4 = bf16[256,512]{1,0:T(8,128)(2,1)S(1)} copy-done((bf16[256,512]{1,0:T(8,128)(2,1)S(1)}, bf16[256,512]{1,0:T(8,128)(2,1)}, u32[]{:S(2)}) %copy-start.4) | copy-done | bytes 262168
  7.6 0.0 copy-start.5
  7.6 0.9 %copy-done.5 = bf16[512,256]{1,0:T(8,128)(2,1)S(1)} copy-done((bf16[512,256]{1,0:T(8,128)(2,1)S(1)}, bf16[512,256]{1,0:T(8,128)(2,1)}, u32[]{:S(2)}) %copy-start.5) | copy-done | bytes 262168
  8.5 41.7 %shard_map.86 = (bf16[256,1024]{1,0:T(8,128)(2,1)S(1)}, f32[64,1024]{1,0:T(8,128)S(1)}) custom-call(s32[16]{0:T(128)S(1)} %select_reduce_fusion.holder_ref, bf16[512,256]{1,0:T(8,128)(2,1)S(1)} %copy-done.5, bf16[256,512]{1,0:T(8,128)(2,1)S(1)} %copy-done.4, bf16[256,512]{1,0:T(8,128)(2,1)S(1)} %copy-done.3, bf16[256,1024]{1,0:T(8,128)(2,1)S(1)} %copy-done.1, ...), custom_call_target="tpu_custom_call" | custom-call | tf_op jit(solution)/shard_map/pallas_call | solution.py:372
  50.3 0.8 %copy.11 = bf16[256,1024]{1,0:T(8,128)(2,1)} copy(bf16[256,1024]{1,0:T(8,128)(2,1)S(1)} %get-tuple-element.4) | data formatting | bytes 1048576
  51.1 0.7 %copy.12 = f32[64,1024]{1,0:T(8,128)} copy(f32[64,1024]{1,0:T(8,128)S(1)} %get-tuple-element.5) | data formatting | bytes 524288
Async XLA Ops:
  1.4 2.2 %copy-start = (f32[1024,1024]{1,0:T(8,128)S(1)}, f32[1024,1024]{1,0:T(8,128)}, u32[]{:S(2)}) copy-start(f32[1024,1024]{1,0:T(8,128)} %taps_ref.1) | copy-start | bytes 12582916
  3.6 1.0 %copy-start.1 = (bf16[256,1024]{1,0:T(8,128)(2,1)S(1)}, bf16[256,1024]{1,0:T(8,128)(2,1)}, u32[]{:S(2)}) copy-start(bf16[256,1024]{1,0:T(8,128)(2,1)} %x_ref.1) | copy-start | bytes 1572868
  4.6 1.0 %copy-start.2 = (bf16[256,1024]{1,0:T(8,128)(2,1)S(1)}, bf16[256,1024]{1,0:T(8,128)(2,1)}, u32[]{:S(2)}) copy-start(bf16[256,1024]{1,0:T(8,128)(2,1)} %g_ref.1) | copy-start | bytes 1572868
  5.7 0.9 %copy-start.3 = (bf16[256,512]{1,0:T(8,128)(2,1)S(1)}, bf16[256,512]{1,0:T(8,128)(2,1)}, u32[]{:S(2)}) copy-start(bf16[256,512]{1,0:T(8,128)(2,1)} %constant.10.clone.back_ref) | copy-start | bytes 786436
  6.6 0.9 %copy-start.4 = (bf16[256,512]{1,0:T(8,128)(2,1)S(1)}, bf16[256,512]{1,0:T(8,128)(2,1)}, u32[]{:S(2)}) copy-start(bf16[256,512]{1,0:T(8,128)(2,1)} %constant.9.clone.inv_ref) | copy-start | bytes 786436
  7.6 0.9 %copy-start.5 = (bf16[512,256]{1,0:T(8,128)(2,1)S(1)}, bf16[512,256]{1,0:T(8,128)(2,1)}, u32[]{:S(2)}) copy-start(bf16[512,256]{1,0:T(8,128)(2,1)} %constant.8.clone.fwd_ref) | copy-start | bytes 786436
where the time goes:
time: 52.1 us; the launch traced here: 51.8 us
  Pallas kernels  41.7 us (80%)
  local copies, waits for them, and re-layouts  8.62 us (17%)
  other arithmetic  0.77 us (1%)
  between operations  0.65 us (1%)
    pallas_call x1, Pallas kernels, shards(): pl.pallas_call(functools.partial(kernel, gang, planes, scale), out_shape=...  41.7 us
    unnamed x14, local copies, waits for them, and re-layouts  8.62 us

commit v1 on v0

v1 whole, which is shorter than its diff:
```python
import functools
import math

import jax
import jax.numpy as jnp
import ml_dtypes
import numpy as np
from jax import lax
from jax.experimental import pallas as pl
from jax.experimental.pallas import tpu as pltpu
from jax.sharding import PartitionSpec as P

MESH = pl.DeviceIdType.MESH
ROWS = 16
HALVES = 2
LANES = 128


def make_tables(block):
    order = np.concatenate([np.arange(0, block, 2), np.arange(1, block, 2)]).astype(np.int64)
    place = np.arange(block, dtype=np.int64)
    period = 4 * block
    ahead = ((2 * order + 1)[:, None] * place[None, :]) % period
    ahead = ahead * (2.0 * math.pi / period)
    forward = np.concatenate([np.cos(ahead), -np.sin(ahead)], axis=0)
    inverse = np.concatenate([np.cos(ahead), -np.sin(ahead)], axis=0).T / block
    return [t.astype(np.float32).astype(ml_dtypes.bfloat16) for t in (forward, inverse)]


def kernel(
    gang,
    planes,
    scale,
    holder_ref,
    fwd_hbm,
    inv_hbm,
    x_ref,
    g_ref,
    taps_ref,
    o_ref,
    f_ref,
    fwd_ref,
    inv_ref,
    xbuf,
    gbuf,
    taps,
    xspec,
    gspec,
    fspec,
    prod,
    lag,
    outbuf,
    lag_send,
    lag_recv,
    lag_sum,
    local_sem,
    own_sem,
    x_send,
    x_recv,
    g_send,
    g_recv,
    gh_send,
    gh_recv,
    o_send,
    o_recv,
    f_send,
    f_recv,
    l_send,
    l_recv,
):
    me = lax.axis_index("ctx")
    q = me // gang
    j = me % gang
    halves, block, width = xbuf.shape[0], xbuf.shape[2], xbuf.shape[3]
    lag_block = f_ref.shape[0]
    half = block // 2

    def peer(d):
        found = 0
        bit = 1
        while bit < gang:
            found = found + ((j // bit + d // bit) % 2) * bit
            bit *= 2
        return found

    def cols(at, h):
        return pl.ds(pl.multiple_of((at * halves + h) * width, width), width)

    def remote(src, dst, send, recv, plane, at):
        return pltpu.make_async_remote_copy(
            src_ref=src,
            dst_ref=dst,
            send_sem=send,
            recv_sem=recv,
            device_id={"ctx": plane * gang + at},
            device_id_type=MESH,
        )

    barrier = pltpu.get_barrier_semaphore()
    for d in range(1, gang):
        pl.semaphore_signal(
            barrier, inc=1, device_id={"ctx": q * gang + peer(d)}, device_id_type=MESH
        )
    for e in range(1, planes):
        pl.semaphore_signal(
            barrier, inc=1, device_id={"ctx": ((q + e) % planes) * gang + j}, device_id_type=MESH
        )

    def own(n, h):
        source, target = [
            (x_ref.at[:, cols(j, h)], xbuf.at[h, j]),
            (g_ref.at[:, cols(j, h)], gbuf.at[h, 0, j]),
            (taps_ref.at[:, cols(j, h)], taps.at[h]),
        ][n]
        return pltpu.make_async_copy(source, target, own_sem.at[n, h])

    fetched = [
        pltpu.make_async_copy(fwd_hbm, fwd_ref, local_sem.at[0]),
        pltpu.make_async_copy(inv_hbm, inv_ref, local_sem.at[1]),
    ]
    fetched[0].start()
    for n in (2, 1, 0):
        for h in range(halves):
            own(n, h).start()
    fetched[1].start()

    pl.semaphore_wait(barrier, gang - 1 + planes - 1)

    def x_copy(h, d):
        return remote(
            x_ref.at[:, cols(peer(d), h)],
            xbuf.at[h, j],
            x_send.at[h, d],
            x_recv.at[h, d],
            q,
            peer(d),
        )

    def g_copy(h, d):
        return remote(
            g_ref.at[:, cols(peer(d), h)],
            gbuf.at[h, 0, j],
            g_send.at[h, d],
            g_recv.at[h, d],
            q,
            peer(d),
        )

    def g_ahead(h, d):
        source = g_ref.at[:, cols(j, h)] if d == 0 else gbuf.at[h, 0, peer(d)]
        return remote(
            source,
            gbuf.at[h, 1, peer(d)],
            gh_send.at[h, d],
            gh_recv.at[h, d],
            (q + planes - 1) % planes,
            j,
        )

    def arrived(ref, sem, at):
        remote(ref, ref, sem, sem, q, at).wait_recv()

    far_first = list(range(gang - 1, 0, -1))

    def send_g(h):
        for d in far_first:
            g_copy(h, d).start()

    def send_x(h):
        for d in far_first:
            x_copy(h, d).start()

    send_g(0)
    send_x(0)
    for h in range(halves):

        @pl.when(q > 0)
        def _():
            g_ahead(h, 0).start()

    @pl.when(q == planes - 1)
    def _():
        for h in range(halves):
            gbuf[h, 1] = jnp.zeros(gbuf.shape[2:], gbuf.dtype)

    def spectrum(value):
        return jnp.dot(fwd_ref[...], value, preferred_element_type=jnp.float32)

    fetched[0].wait()

    for h in range(halves):
        own(2, h).wait()

        @pl.loop(0, gang)
        def _(t):
            rows = pl.ds(pl.multiple_of(t * block, block), block)
            fspec[h, t] = spectrum(taps[h, rows, :].astype(jnp.bfloat16))

    def g_arrive(h):
        for d in range(1, gang):
            arrived(gbuf.at[h, 0, peer(d)], g_recv.at[h, d], peer(d))

            @pl.when(q > 0)
            def _():
                g_ahead(h, d).start()

    def x_arrive(h):
        for d in range(1, gang):
            arrived(xbuf.at[h, peer(d)], x_recv.at[h, d], peer(d))

    def g_spectra(h, side):
        @pl.loop(0, gang)
        def _(t):
            gspec[h, side * gang + t] = spectrum(gbuf[h, side, t])

    def x_spectra(h):
        @pl.loop(0, gang)
        def _(t):
            xspec[h, t] = spectrum(xbuf[h, t])

    def tiles(body):
        for part, sign in ((0, 1.0), (1, -1.0)):
            for lane in range(width // LANES):

                @pl.loop(0, half // ROWS)
                def _(step):
                    first = pl.multiple_of(part * half + step * ROWS, ROWS)
                    second = pl.multiple_of(block + part * half + step * ROWS, ROWS)
                    at = pl.ds(lane * LANES, LANES)
                    body(pl.ds(first, ROWS), pl.ds(second, ROWS), at, sign)

    def windows(h, real, imag, at, sign):
        parts = [(gspec[h, w, real, at], gspec[h, w, imag, at]) for w in range(2 * gang)]
        found = []
        for w in range(2 * gang - 1):
            low, high = parts[w], parts[w + 1]
            if sign > 0:
                found.append((low[0] + high[1], low[1] - high[0]))
            else:
                found.append((low[0] - high[1], low[1] + high[0]))
        return found

    def products(spec, h):
        def body(real, imag, at, sign):
            window = windows(h, real, imag, at, sign)
            lone = [(spec[h, t, real, at], spec[h, t, imag, at]) for t in range(gang)]
            for n in range(gang):
                total_r, total_i = None, None
                for t in range(gang):
                    a, b = lone[t], window[n + t]
                    r = a[0] * b[0] + a[1] * b[1]
                    i = a[0] * b[1] - a[1] * b[0]
                    total_r = r if total_r is None else total_r + r
                    total_i = i if total_i is None else total_i + i
                prod[n, real, at] = total_r.astype(jnp.bfloat16)
                prod[n, imag, at] = total_i.astype(jnp.bfloat16)

        tiles(body)

    def lag_copy(h, e):
        to = (q + e) % planes
        return remote(
            lag_send.at[h, to], lag_recv.at[h, q], l_send.at[h, e], l_recv.at[h, e], to, j
        )

    def lag_part(h):
        @pl.when(q < planes - 1)
        def _():
            for d in range(gang):
                arrived(gbuf.at[h, 1, peer(d)], gh_recv.at[h, d], j)

        g_spectra(h, 1)
        products(xspec, h)

        @pl.loop(0, gang)
        def _(o):
            found = jnp.dot(inv_ref[...], prod[o], preferred_element_type=jnp.float32)
            count = block // lag_block
            lag[pl.ds(o * count, count)] = found.reshape(count, lag_block, width)

        for e in range(planes):
            to = (q + e + 1) % planes
            pieces = []
            for at in range(gang):
                pieces.append(lag[holder_ref[to * gang + at]])
            whole = jnp.concatenate(pieces, axis=0)
            if e < planes - 1:
                lag_send[h, to] = whole.astype(jnp.bfloat16)
                lag_copy(h, e + 1).start()
            else:
                lag_sum[h] = whole

    def o_copy(h, d):
        return remote(
            outbuf.at[h, peer(d)],
            o_ref.at[:, cols(j, h)],
            o_send.at[h, d],
            o_recv.at[h, d],
            q,
            peer(d),
        )

    def own_o(h):
        return pltpu.make_async_copy(outbuf.at[h, j], o_ref.at[:, cols(j, h)], own_sem.at[3, h])

    def grad_part(h):
        products(fspec, h)

        @pl.loop(0, gang)
        def _(t):
            outbuf[h, t] = jnp.dot(
                inv_ref[...], prod[t], preferred_element_type=jnp.float32
            ).astype(jnp.bfloat16)

    def send_o(h):
        for d in far_first:
            o_copy(h, d).start()
        own_o(h).start()

    def lag_rows(h, at):
        return lag_sum.at[h, pl.ds(pl.multiple_of(at * lag_block, lag_block), lag_block), :]

    def f_copy(h, d):
        return remote(
            lag_rows(h, peer(d)),
            f_ref.at[:, cols(j, h)],
            f_send.at[h, d],
            f_recv.at[h, d],
            q,
            peer(d),
        )

    def own_f(h):
        return pltpu.make_async_copy(lag_rows(h, j), f_ref.at[:, cols(j, h)], own_sem.at[4, h])

    def lag_finish(h):
        total = lag_sum[h]
        for e in range(1, planes):
            source = (q + planes - e) % planes
            arrived(lag_recv.at[h, source], l_recv.at[h, e], j)
            total = total + lag_recv[h, source].astype(jnp.float32)
        lag_sum[h] = total * scale
        for d in far_first:
            f_copy(h, d).start()
        own_f(h).start()

    for h in range(halves):
        g_arrive(h)
        if h + 1 < halves:
            send_g(h + 1)
        own(1, h).wait()
        g_spectra(h, 0)
        if h == 0:
            fetched[1].wait()
        else:
            grad_part(h - 1)
        x_arrive(h)
        if h + 1 < halves:
            send_x(h + 1)
        own(0, h).wait()
        x_spectra(h)
        if h > 0:
            send_o(h - 1)
        lag_part(h)
    grad_part(halves - 1)
    send_o(halves - 1)
    for h in range(halves):
        lag_finish(h)

    for h in range(halves):
        for d in range(1, gang):
            arrived(o_ref.at[:, cols(peer(d), h)], o_recv.at[h, d], peer(d))
            arrived(f_ref.at[:, cols(peer(d), h)], f_recv.at[h, d], peer(d))
            x_copy(h, d).wait_send()
            g_copy(h, d).wait_send()
            o_copy(h, d).wait_send()
            f_copy(h, d).wait_send()
        for e in range(1, planes):
            lag_copy(h, e).wait_send()

        @pl.when(q > 0)
        def _():
            for d in range(gang):
                g_ahead(h, d).wait_send()

        own_o(h).wait()
        own_f(h).wait()


def shards(inputs, out_grad, filter_taps, block_owner):
    block, channels = inputs.shape
    devices = lax.axis_size("ctx")
    lags = filter_taps.shape[0]
    gang = lags // block
    planes = devices // gang
    width = channels // gang // HALVES
    lag_block = lags // devices
    scale = 1.0 / math.sqrt(devices * block)
    ids = jnp.arange(devices, dtype=jnp.int32)
    holder = jnp.sum(
        jnp.where(block_owner[None, :] == ids[:, None], ids[None, :], 0), axis=1, dtype=jnp.int32
    )
    forward, inverse = [jnp.asarray(t) for t in make_tables(block)]
    hbm = pl.BlockSpec(memory_space=pltpu.HBM)
    dma = pltpu.SemaphoreType.DMA
    return pl.pallas_call(
        functools.partial(kernel, gang, planes, scale),
        out_shape=(
            jax.ShapeDtypeStruct((block, channels), jnp.bfloat16),
            jax.ShapeDtypeStruct((lag_block, channels), jnp.float32),
        ),
        in_specs=[pl.BlockSpec(memory_space=pltpu.SMEM)] + [hbm] * 5,
        out_specs=(hbm, hbm),
        scratch_shapes=[
            pltpu.VMEM(forward.shape, jnp.bfloat16),
            pltpu.VMEM(inverse.shape, jnp.bfloat16),
            pltpu.VMEM((HALVES, gang, block, width), jnp.bfloat16),
            pltpu.VMEM((HALVES, 2, gang, block, width), jnp.bfloat16),
            pltpu.VMEM((HALVES, lags, width), jnp.float32),
            pltpu.VMEM((HALVES, gang, 2 * block, width), jnp.float32),
            pltpu.VMEM((HALVES, 2 * gang, 2 * block, width), jnp.float32),
            pltpu.VMEM((HALVES, gang, 2 * block, width), jnp.float32),
            pltpu.VMEM((gang, 2 * block, width), jnp.bfloat16),
            pltpu.VMEM((devices, lag_block, width), jnp.float32),
            pltpu.VMEM((HALVES, gang, block, width), jnp.bfloat16),
            pltpu.VMEM((HALVES, planes, gang * lag_block, width), jnp.bfloat16),
            pltpu.VMEM((HALVES, planes, gang * lag_block, width), jnp.bfloat16),
            pltpu.VMEM((HALVES, gang * lag_block, width), jnp.float32),
            dma((2,)),
            dma((5, HALVES)),
        ]
        + [dma((HALVES, gang))] * 10
        + [dma((HALVES, planes))] * 2,
        compiler_params=pltpu.CompilerParams(
            collective_id=0, has_side_effects=True, vmem_limit_bytes=62 * 1024 * 1024
        ),
    )(holder, forward, inverse, inputs, out_grad, filter_taps)


def solution(mesh):
    placed = (P(("groups", "ctx"), None), P(("groups", "ctx"), None), P("groups", None), P())
    return jax.shard_map(
        shards,
        mesh=mesh,
        in_specs=placed,
        out_specs=(P(("groups", "ctx"), None), P(("groups", "ctx"), None)),
        check_vma=False,
    )
```

time: 52.1 us -> 46.3 us (0.89)
  local copies, waits for them, and re-layouts: 8.62 us -> 3.54 us
  Pallas kernels: 41.7 us -> 40.6 us
    unnamed x14 -> x2, local copies, waits for them, and re-layouts: 8.62 us -> 3.54 us
    pallas_call x1, Pallas kernels: 41.7 us -> 40.6 us  [shards(): pl.pallas_call(functools.partial(kernel, gang, planes, scale), out_shape=...]
where the time goes in v1:
time: 46.3 us; the launch traced here: 46 us
  Pallas kernels  40.6 us (88%)
  local copies, waits for them, and re-layouts  3.54 us (8%)
  other arithmetic  1.28 us (3%)
  between operations  0.64 us (1%)
    pallas_call x1, Pallas kernels, shards(): pl.pallas_call(functools.partial(kernel, gang, planes, scale), out_shape=...  40.6 us
    unnamed x2, local copies, waits for them, and re-layouts  3.54 us
    reduce_sum x1, other arithmetic, shards(): jnp.sum(jnp.where(block_owner[None, :] == ids[:, None], ids[None, :], 0),...  1.28 us

profile of v1, /device:TPU:14, one launch (start us, length us, event | category | flops | bytes accessed | tf_op | source)
XLA Modules:
  0.0 46.0 jit_solution(9388206696813796301)
XLA Ops:
  0.6 1.3 %select_reduce_fusion.holder_ref = s32[16]{0:T(128)} fusion(s32[16]{0:T(128)} %param.9), kind=kLoop, calls=%fused_computation | loop fusion | flops 752 | bytes 128 | tf_op jit(solution)/shard_map/reduce_sum | solution.py:400
  1.9 40.6 %shard_map.77 = (bf16[256,1024]{1,0:T(8,128)(2,1)}, f32[64,1024]{1,0:T(8,128)}) custom-call(s32[16]{0:T(128)} %select_reduce_fusion.holder_ref, bf16[512,256]{1,0:T(8,128)(2,1)} %constant.6.clone.fwd_hbm, bf16[256,512]{1,0:T(8,128)(2,1)} %constant.7.clone.inv_hbm, bf16[256,1024]{1,0:T(8,128)(2,1)} %x_ref.1, bf16[256,1024]{1,0:T(8,128)(2,1)} %g_ref.1, ...), custom_call_target="tpu_custom_call" | custom-call | tf_op jit(solution)/shard_map/pallas_call | solution.py:406
  42.5 1.9 %copy.10 = bf16[256,1024]{1,0:T(8,128)(2,1)} copy(bf16[256,1024]{1,0:T(8,128)(2,1)} %get-tuple-element.4) | data formatting | bytes 1048576
  44.4 1.7 %copy.11 = f32[64,1024]{1,0:T(8,128)} copy(f32[64,1024]{1,0:T(8,128)} %get-tuple-element.5) | data formatting | bytes 524288

commit v2 on v1

--- a/solution.py
+++ b/solution.py
@@ -170,8 +170,10 @@
         for d in far_first:
             x_copy(h, d).start()
 
-    send_g(0)
-    send_x(0)
+    for h in range(halves):
+        send_g(h)
+    for h in range(halves):
+        send_x(h)
     for h in range(halves):
 
         @pl.when(q > 0)
@@ -278,15 +280,18 @@
             count = block // lag_block
             lag[pl.ds(o * count, count)] = found.reshape(count, lag_block, width)
 
+        middle = planes // 2
+        hops = sorted(range(1, planes), key=lambda e: abs(e - middle)) + [0]
         for e in range(planes):
-            to = (q + e + 1) % planes
+            hop = hops[e]
+            to = (q + hop) % planes
             pieces = []
             for at in range(gang):
                 pieces.append(lag[holder_ref[to * gang + at]])
             whole = jnp.concatenate(pieces, axis=0)
             if e < planes - 1:
                 lag_send[h, to] = whole.astype(jnp.bfloat16)
-                lag_copy(h, e + 1).start()
+                lag_copy(h, hop).start()
             else:
                 lag_sum[h] = whole
 
@@ -346,8 +351,7 @@
 
     for h in range(halves):
         g_arrive(h)
-        if h + 1 < halves:
-            send_g(h + 1)
+    for h in range(halves):
         own(1, h).wait()
         g_spectra(h, 0)
         if h == 0:
@@ -355,17 +359,16 @@
         else:
             grad_part(h - 1)
         x_arrive(h)
-        if h + 1 < halves:
-            send_x(h + 1)
         own(0, h).wait()
         x_spectra(h)
         if h > 0:
             send_o(h - 1)
         lag_part(h)
+    for h in range(halves - 1):
+        lag_finish(h)
     grad_part(halves - 1)
     send_o(halves - 1)
-    for h in range(halves):
-        lag_finish(h)
+    lag_finish(halves - 1)
 
     for h in range(halves):
         for d in range(1, gang):

time: 46.3 us -> 41.6 us (0.90)
  the two profiles are of different devices: /device:TPU:14 before, /device:TPU:0 now
where the time goes in v2:
time: 41.6 us; the launch traced here: 41.4 us
  Pallas kernels  36 us (87%)
  local copies, waits for them, and re-layouts  3.54 us (9%)
  other arithmetic  1.28 us (3%)
  between operations  0.64 us (2%)
    pallas_call x1, Pallas kernels, shards(): pl.pallas_call(functools.partial(kernel, gang, planes, scale), out_shape=...  36 us
    unnamed x2, local copies, waits for them, and re-layouts  3.54 us
    reduce_sum x1, other arithmetic, shards(): jnp.sum(jnp.where(block_owner[None, :] == ids[:, None], ids[None, :], 0),...  1.28 us

profile of v2, /device:TPU:0, one launch (start us, length us, event | category | flops | bytes accessed | tf_op | source)
XLA Modules:
  0.0 41.4 jit_solution(6761743119409881677)
XLA Ops:
  0.6 1.3 %select_reduce_fusion.holder_ref = s32[16]{0:T(128)} fusion(s32[16]{0:T(128)} %param.9), kind=kLoop, calls=%fused_computation | loop fusion | flops 752 | bytes 128 | tf_op jit(solution)/shard_map/reduce_sum | solution.py:403
  1.9 36.0 %shard_map.77 = (bf16[256,1024]{1,0:T(8,128)(2,1)}, f32[64,1024]{1,0:T(8,128)}) custom-call(s32[16]{0:T(128)} %select_reduce_fusion.holder_ref, bf16[512,256]{1,0:T(8,128)(2,1)} %constant.6.clone.fwd_hbm, bf16[256,512]{1,0:T(8,128)(2,1)} %constant.7.clone.inv_hbm, bf16[256,1024]{1,0:T(8,128)(2,1)} %x_ref.1, bf16[256,1024]{1,0:T(8,128)(2,1)} %g_ref.1, ...), custom_call_target="tpu_custom_call" | custom-call | tf_op jit(solution)/shard_map/pallas_call | solution.py:409
  37.9 1.9 %copy.10 = bf16[256,1024]{1,0:T(8,128)(2,1)} copy(bf16[256,1024]{1,0:T(8,128)(2,1)} %get-tuple-element.4) | data formatting | bytes 1048576
  39.7 1.7 %copy.11 = f32[64,1024]{1,0:T(8,128)} copy(f32[64,1024]{1,0:T(8,128)} %get-tuple-element.5) | data formatting | bytes 524288
